TPU v7x, 256 devices: a whole 4x4x8 slice. The times are simulated.
256 devices in a mesh: row: 32 (over y, z), col: 8 (over x, core).
Axes of the slice: x: 4, y: 4, z: 8, core: 2. Of those that a mesh axis runs over, the one named last changes fastest.
Arguments:
- context: bfloat16 [262144, 512], P(('row', 'col')), may hold values from -6 to 6
- cotangent: bfloat16 [262144, 1024], P(('row', 'col')), may hold values from -0.1875 to 0.1875
- out_weight: bfloat16 [512, 1024], replicated, may hold values from -0.1875 to 0.1875
- momentum: float32 [512, 1024], replicated, may hold values from -6 to 6
- worker_error: float32 [32, 8, 32, 16384], P('row', 'col'), may hold values from -3 to 3
- server_rows: float32 [32, 8, 32, 512], P('row', 'col'), may hold values from -3 to 3
- server_cols: float32 [32, 8, 32, 64], P('row', 'col'), may hold values from -3 to 3
Outputs:
- input_grad: bfloat16 [262144, 512], P(('row', 'col'))
- average: float32 [512, 1024], replicated
- worker_new: float32 [32, 8, 32, 16384], P('row', 'col')
- rows_new: float32 [32, 8, 32, 512], P('row', 'col')
- cols_new: float32 [32, 8, 32, 64], P('row', 'col')
All inputs are finite; a program needn't handle non-finite values.
Results may differ from a plain program's by a relative error of at most 0.025.
Values may be sent and summed in bfloat16 or wider, within the bound.
A program may use at most 64 MiB of HBM per device.

v0:
```python
import jax
import jax.numpy as jnp
from jax import lax
from jax.sharding import PartitionSpec as P


def compress(values):
    scale = jnp.sqrt(jnp.mean(values * values) + 1e-06)
    packed = (scale * jnp.tanh(3.0 * values / scale)).astype(jnp.bfloat16)
    return (packed, values - packed.astype(jnp.float32))


def local(context, cotangent, out_weight, momentum, worker_error, server_rows, server_cols):
    row_count = lax.axis_size("row")
    col_count = lax.axis_size("col")
    lanes = worker_error.shape[2]
    width = worker_error.shape[3]
    grad = lax.dot_general(
        context, cotangent, (((0,), (0,)), ((), ())), preferred_element_type=jnp.float32
    )
    values = (0.9 * momentum + 0.1 * grad).reshape(lanes, width) + worker_error[0, 0]
    sent, worker_new = compress(values)
    received = lax.all_to_all(sent, "row", split_axis=1, concat_axis=0, tiled=True)
    summed = jnp.sum(received.reshape(row_count, lanes, -1).astype(jnp.float32), axis=0)
    input_grad = lax.dot_general(
        cotangent, out_weight, (((1,), (1,)), ((), ())), preferred_element_type=jnp.float32
    ).astype(jnp.bfloat16)
    first = summed / row_count + server_rows[0, 0]
    middle, rows_new = compress(first)
    received_two = lax.all_to_all(middle, "col", split_axis=1, concat_axis=0, tiled=True)
    summed_two = jnp.sum(received_two.reshape(col_count, lanes, -1).astype(jnp.float32), axis=0)
    second = summed_two / col_count + server_cols[0, 0]
    final, cols_new = compress(second)
    partial_block = lax.all_gather(final, "col", axis=1, tiled=True)
    whole = lax.all_gather(partial_block, "row", axis=1, tiled=True)
    average = whole.astype(jnp.float32).reshape(momentum.shape)
    return (input_grad, average, worker_new[None, None], rows_new[None, None], cols_new[None, None])


def solution(mesh):
    in_specs = (
        P(("row", "col"), None),
        P(("row", "col"), None),
        P(),
        P(),
        P("row", "col", None, None),
        P("row", "col", None, None),
        P("row", "col", None, None),
    )
    out_specs = (
        P(("row", "col"), None),
        P(),
        P("row", "col", None, None),
        P("row", "col", None, None),
        P("row", "col", None, None),
    )
    return jax.shard_map(local, mesh=mesh, in_specs=in_specs, out_specs=out_specs, check_vma=False)
```

profile of v0, /device:TPU:2, one launch (start us, length us, event | category | flops | bytes accessed | tf_op | source)
XLA Modules:
  0.0 167.0 jit_solution(11059005104408429845)
XLA Ops:
  7.2 0.0 copy-start
  7.2 0.0 copy-start.4
  7.2 2.9 %squeeze.13 = f32[512,1024]{1,0:T(8,128)} reshape(f32[1,1,32,16384]{3,2,1,0:T(8,128)} %param.11) | data formatting | bytes 4194304 | tf_op jit(solution)/shard_map/squeeze | solution.py:21
  10.1 0.0 copy-done
  10.1 0.0 copy-done.4
  10.1 5.5 %multiply_reduce_fusion = (f32[]{:T(128)}, f32[512,1024]{1,0:T(8,128)}) fusion(f32[512,1024]{1,0:T(8,128)} %squeeze.13, bf16[1024,512]{1,0:T(8,128)(2,1)S(1)} %copy-done.4, bf16[1024,1024]{1,0:T(8,128)(2,1)S(1)} %copy-done, f32[512,1024]{1,0:T(8,128)} %param.10), kind=kOutput, calls=%fused_computation.8 | convolution fusion | flops 1076887552 | bytes 9437188 | tf_op jit(solution)/shard_map/dot_general | solution.py:18
  15.6 2.7 %reshape.57 = f32[32,32,512]{2,1,0:T(8,128)} reshape(f32[512,1024]{1,0:T(8,128)} %get-tuple-element.8) | data formatting | bytes 4194304 | tf_op jit(solution)/shard_map/reshape | solution.py:21
  19.0 0.0 copy-start.1
  19.0 3.0 %copy.18 = f32[4,8,32,512]{3,2,1,0:T(8,128)S(1)} copy(f32[4,8,32,512]{3,1,2,0:T(8,128)} %bitcast.55) | data formatting | bytes 4194304
  22.0 0.0 copy-done.1
  22.0 0.6 fusion.4
  22.6 0.0 copy-start.2
  22.6 1.5 copy.15
  24.2 11.5 %all-to-all-start = ((bf16[32,32,512]{2,0,1:T(8,128)(2,1)}), bf16[32,32,512]{2,0,1:T(8,128)(2,1)S(1)}, u32[]{:S(2)}, u32[]{:S(2)}) async-start(bf16[32,32,512]{2,0,1:T(8,128)(2,1)} %copy.15), calls=%async_computation | async-start | bytes 2097152 | tf_op jit(solution)/shard_map/all_to_all | solution.py:23
  35.7 0.0 copy-done.2
  35.7 0.1 squeeze.16
  35.8 28.5 %all-to-all-done = bf16[32,32,512]{2,0,1:T(8,128)(2,1)S(1)} async-done(((bf16[32,32,512]{2,0,1:T(8,128)(2,1)}), bf16[32,32,512]{2,0,1:T(8,128)(2,1)S(1)}, u32[]{:S(2)}, u32[]{:S(2)}) %all-to-all-start) | async-done | bytes 1048608 | tf_op jit(solution)/shard_map/all_to_all | solution.py:23
  64.3 0.2 convert_reduce_fusion
  64.4 0.6 fusion.6
  65.8 0.1 div.55
  65.9 0.7 reshape.65
  66.6 4.8 %all-to-all-start.1 = ((bf16[8,2,1024]{2,1,0:T(2,128)(2,1)}), bf16[8,2,1024]{2,1,0:T(2,128)(2,1)S(1)}, u32[]{:S(2)}, u32[]{:S(2)}) async-start(bf16[8,2,1024]{2,1,0:T(2,128)(2,1)} %reshape.65), calls=%async_computation.1 | async-start | bytes 65536 | tf_op jit(solution)/shard_map/all_to_all | solution.py:30
  71.5 0.0 copy-start.3
  71.5 0.0 all-gather.3.cloned.1.call-start
  71.5 2.7 %reshape.60 = f32[1,1,32,16384]{3,2,1,0:T(8,128)} reshape(f32[512,1024]{1,0:T(8,128)} %get-tuple-element.8) | data formatting | bytes 4194304 | tf_op jit(solution)/shard_map/reshape | solution.py:21
  74.2 1.2 all-to-all-done.1
  75.5 0.1 reshape.66
  75.6 0.0 copy-done.3
  75.6 0.6 multiply_reduce_fusion.1
  76.9 12.2 %all-gather = bf16[8,64,32]{1,2,0:T(8,128)(2,1)S(1)} all-gather(bf16[1,64,32]{1,2,0:T(8,128)(2,1)S(1)} %fusion.7), channel_id=1, replica_groups=mesh['row'=32,'col'=8] {'col'}, dimensions={0}, use_global_device_ids=true | all-gather | bytes 36864 | tf_op jit(solution)/shard_map/all_gather | solution.py:34
  89.1 0.7 reshape.64
  89.9 0.0 all-gather.3.cloned.1.call-update
  89.9 0.0 copy-start.5
  89.9 4.0 %convert_subtract_fusion = f32[1,1,32,16384]{3,2,1,0:T(8,128)} fusion(f32[1,1,32,16384]{3,2,1,0:T(8,128)} %reshape.60, f32[1,1,32,16384]{3,2,1,0:T(8,128)} %param.11, f32[]{:T(128)S(6)} %sqrt.9), kind=kLoop, calls=%fused_computation.5 | loop fusion | flops 3670016 | bytes 6291460 | tf_op jit(solution)/shard_map/sub | solution.py:10
  93.9 0.0 copy-done.5
  93.9 2.3 %convolution_convert_fusion = bf16[1024,512]{1,0:T(8,128)(2,1)} fusion(bf16[1024,1024]{1,0:T(8,128)(2,1)S(1)} %copy-done, bf16[512,1024]{1,0:T(8,128)(2,1)S(1)} %copy-done.5), kind=kOutput, calls=%fused_computation.11 | convolution fusion | flops 1074266112 | bytes 4194304 | tf_op jit(solution)/shard_map/dot_general | solution.py:25
  96.2 0.7 convert_subtract_fusion.1
  96.8 0.6 convert_subtract_fusion.2
  97.5 60.1 %all-gather.3.cloned.1.call-done = bf16[32,16384]{1,0:T(8,128)(2,1)} async-done(((bf16[32,512]{1,0:T(8,128)(2,1)}), bf16[32,16384]{1,0:T(8,128)(2,1)}) %all-gather.3.cloned.1.call-update) | async-done | bytes 1048592 | tf_op jit(solution)/shard_map/all_gather | solution.py:35
  157.6 2.6 %reshape.62 = f32[512,1024]{1,0:T(8,128)} reshape(bf16[32,16384]{1,0:T(8,128)(2,1)} %all-gather.3.cloned.1.call-done) | data formatting | bytes 3145728 | tf_op jit(solution)/shard_map/reshape | solution.py:36
  (5 shorter events, 0.1 us)
Async XLA Ops:
  7.2 2.9 %copy-start = (bf16[1024,1024]{1,0:T(8,128)(2,1)S(1)}, bf16[1024,1024]{1,0:T(8,128)(2,1)}, u32[]{:S(2)}) copy-start(bf16[1024,1024]{1,0:T(8,128)(2,1)} %param.8) | copy-start | bytes 6291460
  7.2 2.9 %copy-start.4 = (bf16[1024,512]{1,0:T(8,128)(2,1)S(1)}, bf16[1024,512]{1,0:T(8,128)(2,1)}, u32[]{:S(2)}) copy-start(bf16[1024,512]{1,0:T(8,128)(2,1)} %param.7) | copy-start | bytes 3145732
  19.0 3.0 %copy-start.1 = (f32[32,32,512]{2,1,0:T(8,128)S(1)}, f32[32,32,512]{2,1,0:T(8,128)}, u32[]{:S(2)}) copy-start(f32[32,32,512]{2,1,0:T(8,128)} %reshape.57) | copy-start | bytes 6291460
  22.6 13.1 %copy-start.2 = (f32[1,1,32,512]{3,2,1,0:T(8,128)S(1)}, f32[1,1,32,512]{3,2,1,0:T(8,128)}, u32[]{:S(2)}) copy-start(f32[1,1,32,512]{3,2,1,0:T(8,128)} %param.12) | copy-start | bytes 196612
  24.2 40.1 %all-to-all-start = ((bf16[32,32,512]{2,0,1:T(8,128)(2,1)}), bf16[32,32,512]{2,0,1:T(8,128)(2,1)S(1)}, u32[]{:S(2)}, u32[]{:S(2)}) async-start(bf16[32,32,512]{2,0,1:T(8,128)(2,1)} %copy.15), calls=%async_computation | async-start | bytes 2097152 | tf_op jit(solution)/shard_map/all_to_all | solution.py:23
  66.6 8.8 %all-to-all-start.1 = ((bf16[8,2,1024]{2,1,0:T(2,128)(2,1)}), bf16[8,2,1024]{2,1,0:T(2,128)(2,1)S(1)}, u32[]{:S(2)}, u32[]{:S(2)}) async-start(bf16[8,2,1024]{2,1,0:T(2,128)(2,1)} %reshape.65), calls=%async_computation.1 | async-start | bytes 65536 | tf_op jit(solution)/shard_map/all_to_all | solution.py:30
  71.5 4.1 %copy-start.3 = (f32[1,1,32,64]{3,2,1,0:T(8,128)S(1)}, f32[1,1,32,64]{3,2,1,0:T(8,128)}, u32[]{:S(2)}) copy-start(f32[1,1,32,64]{3,2,1,0:T(8,128)} %param.13) | copy-start | bytes 24580
  71.5 86.1 %all-gather.3.cloned.1.call-start = ((), (), s32[]{:S(2)}) async-start(), calls=%async_computation.2 | async-start | bytes 1081344 | tf_op jit(solution)/shard_map/all_gather | solution.py:35
  89.9 4.1 %copy-start.5 = (bf16[512,1024]{1,0:T(8,128)(2,1)S(1)}, bf16[512,1024]{1,0:T(8,128)(2,1)}, u32[]{:S(2)}) copy-start(bf16[512,1024]{1,0:T(8,128)(2,1)} %param.9) | copy-start | bytes 3145732
Sparse Core Ops, SparseCore 0:
  90.0 67.5 all-gather.2
where the time goes:
time: 167 us
  waiting for transfers between devices  89.9 us (54%)
  local copies, waits for them, and re-layouts  17.2 us (10%)
  starting transfers between devices  16.3 us (10%)
  between operations  16.2 us (10%)
  blocking collectives  12.2 us (7%)
  matrix products  7.79 us (5%)
  other arithmetic  7.35 us (4%)
    all_gather x1, waiting for transfers between devices, local(): whole = lax.all_gather(partial_block, 'row', axis=1, tiled=True)  60.1 us
    all_to_all x1, waiting for transfers between devices, local(): lax.all_to_all(sent, 'row', split_axis=1, concat_axis=0, tiled=True)  28.5 us
    all_gather x1, blocking collectives, local(): partial_block = lax.all_gather(final, 'col', axis=1, tiled=True)  12.2 us
    all_to_all x1, starting transfers between devices, local(): lax.all_to_all(sent, 'row', split_axis=1, concat_axis=0, tiled=True)  11.5 us
    dot_general x1, matrix products, local(): lax.dot_general(context, cotangent, (((0,), (0,)), ((), ())), preferred_e...  5.53 us
    reshape x2, local copies, waits for them, and re-layouts, local(): (0.9 * momentum + 0.1 * grad).reshape(lanes, width) + worker_error[0, 0]  5.46 us
    sub x3, other arithmetic, compress(): return (packed, values - packed.astype(jnp.float32))  5.32 us
    all_to_all x1, starting transfers between devices, local(): lax.all_to_all(middle, 'col', split_axis=1, concat_axis=0, tiled=True)  4.83 us
  transfers between devices with their start and end apart: 3, of which 3 were waited for; matrix products, arithmetic and copies ran while one was open for 6% of the time, Pallas kernels for 0%

commit v1 on v0

v1 whole, which is shorter than its diff:
```python
import functools

import jax
import jax.numpy as jnp
from jax import lax
from jax.experimental import pallas as pl
from jax.experimental.pallas import tpu as pltpu
from jax.sharding import PartitionSpec as P

MESH = pl.DeviceIdType.MESH
F32, BF16 = jnp.float32, jnp.bfloat16

NX, NY, NZ, NC = 4, 4, 8, 2
LANES, WIDTH = 32, 16384
BLOCK = 512
YC = 384
ZC = BLOCK - YC
ROWS = 16


def place():
    row, col = lax.axis_index("row"), lax.axis_index("col")
    return col // NC, row // NZ, lax.rem(row, NZ), lax.rem(col, NC)


def device(x, y, z, c):
    return (y * NZ + z, x * NC + c)


def scale_of(total, count):
    return jnp.sqrt(total / count + 1e-06)


def total_of(values):
    return jnp.sum(jnp.sum(values, axis=0, keepdims=True), axis=1, keepdims=True)


def compress(values):
    scale = scale_of(total_of(values * values), values.size)
    packed = (scale * jnp.tanh(values * (3.0 / scale))).astype(BF16)
    return packed, values - packed.astype(F32)


def partners():
    found = [(0, d, 0, 0) for d in range(1, NY)]
    found += [(0, 0, d, 0) for d in range(1, NZ)]
    found += [(dx, 0, 0, dc) for dx in range(NX) for dc in range(NC) if dx or dc]
    found += [(dx, dy, 0, 0) for dx in range(1, NX) for dy in range(1, NY)]
    return found


def fused(
    ctx_h, cot_h, w_h, mom_h, we_h, sr_h, sc_h,
    g_h, wn_h, ig_h, rn_h, cn_h,
    ctx, cot, w, mom, we, sr, sc, ctx_t, grad, vals, ig, rn, cn,
    send_y, got_y, send_z, got_z, part_y, got_y2, part_z, got_z2,
    mid, got_c, fin, gat,
    in_sem, out_sem, wn_sem,
    y_s, y_r, z_s, z_r, y2_s, y2_r, z2_s, z2_r, c_s, c_r, f_s, f_r, p_s, p_r, b_s, b_r,
):
    x, y, z, c = place()

    barrier = pltpu.get_barrier_semaphore()
    known = partners()
    for dx, dy, dz, dc in known:
        there = device(lax.rem(x + dx, NX), lax.rem(y + dy, NY), lax.rem(z + dz, NZ), lax.rem(c + dc, NC))
        pl.semaphore_signal(barrier, inc=1, device_id=there, device_id_type=MESH)

    loads = [
        pltpu.make_async_copy(src, dst, in_sem.at[i])
        for i, (src, dst) in enumerate(
            [(ctx_h, ctx), (cot_h, cot), (w_h, w), (we_h.at[0, 0], we), (sr_h.at[0, 0], sr), (sc_h.at[0, 0], sc)]
            + [(mom_h.at[:, pl.ds(128 * k, 128)], mom.at[k]) for k in range(8)]
        )
    ]
    for load in loads:
        load.start()

    loads[0].wait()
    ctx_t[...] = ctx[...].T
    loads[1].wait()

    @pl.loop(0, 4)
    def _(n):
        cols = pl.ds(pl.multiple_of(n * 256, 256), 256)
        product = jnp.dot(ctx_t[...], cot[:, cols], preferred_element_type=F32)
        grad[2 * n] = product[:, :128]
        grad[2 * n + 1] = product[:, 128:]

    for load in loads[3:4] + loads[6:]:
        load.wait()

    def accumulate(q, total):
        rows = pl.ds(q, LANES, stride=ROWS)
        for k in range(8):
            cols = pl.ds(pl.multiple_of(q * 1024 + 128 * k, 128), 128)
            v = 0.9 * mom[k, rows, :] + 0.1 * grad[k, rows, :] + we[:, cols]
            vals[q, :, 128 * k : 128 * k + 128] = v
            v = v * v
            total = total + (v[0:8] + v[8:16]) + (v[16:24] + v[24:32])
        return total

    total = lax.fori_loop(0, ROWS, accumulate, jnp.zeros((8, 128), F32))
    scale = scale_of(total_of(total), LANES * WIDTH)
    slope = 3.0 / scale

    def soft(v):
        return (scale * jnp.tanh(v * slope)).astype(BF16)

    @pl.loop(0, ROWS)
    def _(q):
        for half in range(2):
            b = 2 * q + half
            cols = pl.ds(half * BLOCK + YC, ZC)
            v = vals[q, :, cols]
            p = soft(v)
            send_z[lax.rem(b, NZ), b // NZ] = p
            vals[q, :, cols] = v - p.astype(F32)

    pl.semaphore_wait(barrier, len(known))

    z_copies = []
    for d in (4, 3, 5, 2, 6, 1, 7):
        to = lax.rem(z + d, NZ)
        copy = pltpu.make_async_remote_copy(
            src_ref=send_z.at[to], dst_ref=got_z.at[z], send_sem=z_s.at[d], recv_sem=z_r.at[d],
            device_id=device(x, y, to, c), device_id_type=MESH,
        )
        copy.start()
        z_copies.append(copy)
    got_z[z] = send_z[z]

    y_copies, wn_copies = {}, []
    for e in (2, 1, 3, 0):
        k = lax.rem(z // 2 + e, NZ // 2)
        for d in (2, 1, 3, 0):
            to = lax.rem(y + d, NY)
            q = to * 4 + k
            for half in range(2):
                cols = pl.ds(half * BLOCK, YC)
                v = vals[q, :, cols]
                p = soft(v)
                if d:
                    send_y[to, 2 * k + half] = p
                else:
                    got_y[y, 2 * k + half] = p
                vals[q, :, cols] = v - p.astype(F32)
            if d:
                pair = pl.ds(2 * k, 2)
                copy = pltpu.make_async_remote_copy(
                    src_ref=send_y.at[to, pair], dst_ref=got_y.at[y, pair], send_sem=y_s.at[e, d], recv_sem=y_r.at[e, d],
                    device_id=device(x, to, z, c), device_id_type=MESH,
                )
                copy.start()
                y_copies[e, d] = copy
            copy = pltpu.make_async_copy(
                vals.at[q], wn_h.at[:, pl.ds(pl.multiple_of(q * 1024, 1024), 1024)], wn_sem.at[4 * e + d]
            )
            copy.start()
            wn_copies.append(copy)

    loads[2].wait()

    @pl.loop(0, 4)
    def _(n):
        rows = pl.ds(pl.multiple_of(n * 256, 256), 256)
        ig[rows, :] = lax.dot_general(
            cot[rows, :], w[...], (((1,), (1,)), ((), ())), preferred_element_type=F32
        ).astype(BF16)

    ig_copy = pltpu.make_async_copy(ig, ig_h, out_sem.at[0])
    ig_copy.start()

    def add(parts):
        total = parts[0].astype(F32)
        for part in parts[1:]:
            total = total + part.astype(F32)
        return total

    y2_copies = []

    def send_part(to):
        d = lax.rem(to - z + NZ, NZ)
        copy = pltpu.make_async_remote_copy(
            src_ref=part_y.at[to], dst_ref=got_y2.at[z], send_sem=y2_s.at[d], recv_sem=y2_r.at[d],
            device_id=device(x, y, to, c), device_id_type=MESH,
        )
        copy.start()
        y2_copies.append(copy)

    def sum_y(at):
        return add([got_y[i, at] for i in range(NY)]).astype(BF16)

    for e in (2, 1, 3):
        for d in (2, 1, 3):
            y_copies[e, d].wait_recv()
        k = lax.rem(z // 2 + e, NZ // 2)
        for half in range(2):
            part_y[2 * k + half] = sum_y(2 * k + half)
            send_part(2 * k + half)

    for copy in z_copies:
        copy.wait_recv()
    z2_copies = []
    for d in (2, 1, 3, 0):
        to = lax.rem(y + d, NY)
        part = add([got_z[i, to] for i in range(NZ)]).astype(BF16)
        if d:
            part_z[to] = part
            copy = pltpu.make_async_remote_copy(
                src_ref=part_z.at[to], dst_ref=got_z2.at[y], send_sem=z2_s.at[d], recv_sem=z2_r.at[d],
                device_id=device(x, to, z, c), device_id_type=MESH,
            )
            copy.start()
            z2_copies.append(copy)
        else:
            got_z2[y] = part

    for d in (2, 1, 3):
        y_copies[0, d].wait_recv()
    other = z + 1 - 2 * lax.rem(z, 2)
    part_y[other] = sum_y(other)
    send_part(other)
    got_y2[z] = sum_y(z)

    loads[4].wait()
    loads[5].wait()
    for copy in z2_copies:
        copy.wait_recv()
    for d in (4, 3, 5, 2, 6, 1, 7):
        pltpu.make_async_remote_copy(
            src_ref=part_y.at[0], dst_ref=got_y2.at[0], send_sem=y2_s.at[d], recv_sem=y2_r.at[d],
            device_id=device(x, y, lax.rem(z + d, NZ), c), device_id_type=MESH,
        ).wait_recv()
    first = jnp.concatenate(
        [add([got_y2[i] for i in range(NZ)]), add([got_z2[i] for i in range(NY)])], axis=1
    ) * (1.0 / (NY * NZ)) + sr[...]
    middle, rest = compress(first)

    low = lax.broadcasted_iota(jnp.int32, (ROWS, 128), 1) < 64

    def fold(top, bottom):
        return (
            jnp.where(low, top, pltpu.roll(bottom, 64, axis=1)),
            jnp.where(low, pltpu.roll(top, 64, axis=1), bottom),
        )

    middle = middle.astype(F32)
    for k in range(NX):
        group = middle[:, 128 * k : 128 * k + 128]
        even, odd = fold(group[:16], group[16:])
        mid[2 * k] = even.astype(BF16)
        mid[2 * k + 1] = odd.astype(BF16)
    c_copies = []
    for dx in (2, 1, 3, 0):
        for dc in range(NC):
            if dx or dc:
                tx, tc = lax.rem(x + dx, NX), lax.rem(c + dc, NC)
                copy = pltpu.make_async_remote_copy(
                    src_ref=mid.at[2 * tx + tc], dst_ref=got_c.at[2 * x + c],
                    send_sem=c_s.at[2 * dx + dc], recv_sem=c_r.at[2 * dx + dc],
                    device_id=device(tx, y, z, tc), device_id_type=MESH,
                )
                copy.start()
                c_copies.append(copy)
    got_c[2 * x + c] = mid[2 * x + c]
    rn[...] = rest
    rn_copy = pltpu.make_async_copy(rn, rn_h, out_sem.at[1])
    rn_copy.start()
    side = jnp.concatenate([sc[0:16, :], sc[16:32, :]], axis=1)
    for copy in c_copies:
        copy.wait_recv()
    second = add([got_c[i] for i in range(NX * NC)]) * (1.0 / (NX * NC)) + side
    final, rest = compress(second)

    fin[...] = final
    f_copies = []
    for d in (4, 3, 5, 2, 6, 1, 7):
        copy = pltpu.make_async_remote_copy(
            src_ref=fin, dst_ref=gat.at[c, y, x, z], send_sem=f_s.at[d], recv_sem=f_r.at[d],
            device_id=device(x, y, lax.rem(z + d, NZ), c), device_id_type=MESH,
        )
        copy.start()
        f_copies.append(copy)
    gat[c, y, x, z] = final
    cn[0:16, :] = rest[:, 0:64]
    cn[16:32, :] = pltpu.roll(rest, 64, axis=1)[:, 0:64]
    cn_copy = pltpu.make_async_copy(cn, cn_h, out_sem.at[2])
    cn_copy.start()
    for copy in f_copies:
        copy.wait_recv()

    p_copies, b_copies = [], []

    def to_sibling(dx, dy):
        sx, sy = lax.rem(x - dx + NX, NX), lax.rem(y - dy + NY, NY)
        copy = pltpu.make_async_remote_copy(
            src_ref=gat.at[c, sy, sx], dst_ref=gat.at[c, sy, sx],
            send_sem=b_s.at[dx, dy], recv_sem=b_r.at[dx, dy],
            device_id=device(x, y, z, 1 - c), device_id_type=MESH,
        )
        copy.start()
        b_copies.append(copy)

    order = sorted(
        [(dx, dy) for dx in range(NX) for dy in range(NY) if dx or dy],
        key=lambda d: -(min(d[0], NX - d[0]) + min(d[1], NY - d[1])),
    )
    for dx, dy in order:
        copy = pltpu.make_async_remote_copy(
            src_ref=gat.at[c, y, x], dst_ref=gat.at[c, y, x],
            send_sem=p_s.at[dx, dy], recv_sem=p_r.at[dx, dy],
            device_id=device(lax.rem(x + dx, NX), lax.rem(y + dy, NY), z, c), device_id_type=MESH,
        )
        copy.start()
        p_copies.append(((dx, dy), copy))
    to_sibling(0, 0)
    for (dx, dy), copy in reversed(p_copies):
        copy.wait_recv()
        to_sibling(dx, dy)
    for copy in b_copies:
        copy.wait_recv()
    g_copy = pltpu.make_async_copy(gat, g_h, out_sem.at[3])
    g_copy.start()

    for copy in z_copies + list(y_copies.values()) + z2_copies + y2_copies + c_copies + f_copies + b_copies:
        copy.wait_send()
    for _, copy in p_copies:
        copy.wait_send()
    for copy in wn_copies + [ig_copy, rn_copy, cn_copy, g_copy]:
        copy.wait()


def finish(g, wn, ig, rn, cn, avg, wn_out, ig_out, rn_out, cn_out):
    low = lax.broadcasted_iota(jnp.int32, (ROWS, 128), 1) < 64
    for y in range(NY):
        for h in range(NZ // 2):
            even = g[0, y, 0, h, 0].astype(F32)
            odd = g[1, y, 0, h, 0].astype(F32)
            q = y * 4 + h
            avg[pl.ds(q, 16, stride=ROWS), :] = jnp.where(low, even, pltpu.roll(odd, 64, axis=1))
            avg[pl.ds(256 + q, 16, stride=ROWS), :] = jnp.where(low, pltpu.roll(even, 64, axis=1), odd)
    wn_out[0, 0] = wn[...]
    ig_out[...] = ig[...]
    rn_out[0, 0] = rn[...]
    cn_out[0, 0] = cn[...]


def local(context, cotangent, out_weight, momentum, worker_error, server_rows, server_cols):
    anywhere = pl.BlockSpec(memory_space=pl.ANY)
    dma = pltpu.SemaphoreType.DMA
    g, wn, ig, rn, cn = pl.pallas_call(
        fused,
        out_shape=(
            jax.ShapeDtypeStruct((NC, NY, NX, NZ, 16, 128), BF16),
            jax.ShapeDtypeStruct((LANES, WIDTH), F32),
            jax.ShapeDtypeStruct((1024, 512), BF16),
            jax.ShapeDtypeStruct((LANES, BLOCK), F32),
            jax.ShapeDtypeStruct((LANES, 64), F32),
        ),
        in_specs=[pl.BlockSpec(memory_space=pltpu.HBM)] * 7,
        out_specs=[anywhere] * 5,
        scratch_shapes=[
            pltpu.VMEM((1024, 512), BF16),
            pltpu.VMEM((1024, 1024), BF16),
            pltpu.VMEM((512, 1024), BF16),
            pltpu.VMEM((8, 512, 128), F32),
            pltpu.VMEM((LANES, WIDTH), F32),
            pltpu.VMEM((LANES, BLOCK), F32),
            pltpu.VMEM((LANES, 64), F32),
            pltpu.VMEM((512, 1024), BF16),
            pltpu.VMEM((8, 512, 128), F32),
            pltpu.VMEM((ROWS, LANES, 1024), F32),
            pltpu.VMEM((1024, 512), BF16),
            pltpu.VMEM((LANES, BLOCK), F32),
            pltpu.VMEM((LANES, 64), F32),
            pltpu.VMEM((NY, NZ, LANES, YC), BF16),
            pltpu.VMEM((NY, NZ, LANES, YC), BF16),
            pltpu.VMEM((NZ, NY, LANES, ZC), BF16),
            pltpu.VMEM((NZ, NY, LANES, ZC), BF16),
            pltpu.VMEM((NZ, LANES, YC), BF16),
            pltpu.VMEM((NZ, LANES, YC), BF16),
            pltpu.VMEM((NY, LANES, ZC), BF16),
            pltpu.VMEM((NY, LANES, ZC), BF16),
            pltpu.VMEM((NX * NC, 16, 128), BF16),
            pltpu.VMEM((NX * NC, 16, 128), BF16),
            pltpu.VMEM((16, 128), BF16),
            pltpu.VMEM((NC, NY, NX, NZ, 16, 128), BF16),
            dma((14,)), dma((4,)), dma((16,)),
            dma((4, NY)), dma((4, NY)), dma((NZ,)), dma((NZ,)),
            dma((NZ,)), dma((NZ,)), dma((NY,)), dma((NY,)),
            dma((NX * NC,)), dma((NX * NC,)), dma((NZ,)), dma((NZ,)),
            dma((NX, NY)), dma((NX, NY)), dma((NX, NY)), dma((NX, NY)),
        ],
        compiler_params=pltpu.CompilerParams(
            collective_id=0, has_side_effects=True, vmem_limit_bytes=60 << 20
        ),
        cost_estimate=pl.CostEstimate(flops=2 << 30, bytes_accessed=13 << 20, transcendentals=1 << 19),
        name="fused",
    )(context, cotangent, out_weight, momentum, worker_error, server_rows, server_cols)
    return pl.pallas_call(
        finish,
        grid=(8,),
        out_shape=(
            jax.ShapeDtypeStruct((512, 1024), F32),
            jax.ShapeDtypeStruct((1, 1, LANES, WIDTH), F32),
            jax.ShapeDtypeStruct((1024, 512), BF16),
            jax.ShapeDtypeStruct((1, 1, LANES, BLOCK), F32),
            jax.ShapeDtypeStruct((1, 1, LANES, 64), F32),
        ),
        in_specs=[
            pl.BlockSpec((NC, NY, 1, NZ // 2, 1, 16, 128), lambda j: (0, 0, lax.rem(j, 4), 0, j // 4, 0, 0)),
            pl.BlockSpec((LANES, WIDTH // 8), lambda j: (0, j)),
            pl.BlockSpec((128, 512), lambda j: (j, 0)),
            pl.BlockSpec((LANES, 128), lambda j: (0, j // 2)),
            pl.BlockSpec((LANES, 64), lambda j: (0, 0)),
        ],
        out_specs=[
            pl.BlockSpec((512, 128), lambda j: (0, j)),
            pl.BlockSpec((1, 1, LANES, WIDTH // 8), lambda j: (0, 0, 0, j)),
            pl.BlockSpec((128, 512), lambda j: (j, 0)),
            pl.BlockSpec((1, 1, LANES, 128), lambda j: (0, 0, 0, j // 2)),
            pl.BlockSpec((1, 1, LANES, 64), lambda j: (0, 0, 0, 0)),
        ],
        compiler_params=pltpu.CompilerParams(vmem_limit_bytes=60 << 20),
        cost_estimate=pl.CostEstimate(flops=1 << 20, bytes_accessed=9 << 20, transcendentals=0),
        name="finish",
    )(g.reshape(NC, NY, NX, NZ // 2, 2, 16, 128), wn, ig, rn, cn)


def solution(mesh):
    state = P("row", "col", None, None)
    tokens = P(("row", "col"), None)

    def body(*args):
        avg, wn, ig, rn, cn = local(*args)
        return ig, avg, wn, rn, cn

    return jax.shard_map(
        body,
        mesh=mesh,
        in_specs=(tokens, tokens, P(), P(), state, state, state),
        out_specs=(tokens, P(), state, state, state),
        check_vma=False,
    )
```

time: 167 us -> 56.4 us (0.34)
  the two profiles are of different devices: /device:TPU:2 before, /device:TPU:1 now
where the time goes in v1:
time: 56.4 us; the launch traced here: 56.1 us
  Pallas kernels  55.5 us (98%)
  between operations  0.64 us (1%)
    pallas_call x1, Pallas kernels, local(): pl.pallas_call(fused, out_shape=(jax.ShapeDtypeStruct((NC, NY, NX, NZ, 16...  48.6 us
    pallas_call x1, Pallas kernels, local(): pl.pallas_call(finish, grid=(8,), out_shape=(jax.ShapeDtypeStruct((512, 1...  6.89 us

profile of v1, /device:TPU:1, one launch (start us, length us, event | category | flops | bytes accessed | tf_op | source)
XLA Modules:
  0.0 56.1 jit_solution(16915946801406708112)
XLA Ops:
  0.6 48.6 %fused.1 = (bf16[2,4,4,8,16,128]{5,4,3,2,1,0:T(8,128)(2,1)}, f32[32,16384]{1,0:T(8,128)}, bf16[1024,512]{1,0:T(8,128)(2,1)}, f32[32,512]{1,0:T(8,128)}, f32[32,64]{1,0:T(8,128)}) custom-call(bf16[1024,512]{1,0:T(8,128)(2,1)} %ctx_h.1, bf16[1024,1024]{1,0:T(8,128)(2,1)} %cot_h.1, bf16[512,1024]{1,0:T(8,128)(2,1)} %w_h.1, f32[512,1024]{1,0:T(8,128)} %mom_h.1, ...), custom_call_target="tpu_custom_call" | custom-call | flops 2147483648 | bytes 13631488 | tf_op jit(solution)/shard_map/fused/pallas_call | solution.py:352
  49.2 6.9 %finish.1 = (f32[512,1024]{1,0:T(8,128)}, f32[1,1,32,16384]{3,2,1,0:T(8,128)}, bf16[1024,512]{1,0:T(8,128)(2,1)}, f32[1,1,32,512]{3,2,1,0:T(8,128)}, f32[1,1,32,64]{3,2,1,0:T(8,128)}) custom-call(bf16[2,4,4,4,2,16,128]{6,5,4,3,2,1,0:T(8,128)(2,1)} %bitcast.1, f32[32,16384]{1,0:T(8,128)} %get-tuple-element.16.wn, bf16[1024,512]{1,0:T(8,128)(2,1)} %get-tuple-element.17.ig, ...), custom_call_target="tpu_custom_call" | custom-call | flops 1048576 | bytes 9437184 | tf_op jit(solution)/shard_map/finish/pallas_call | solution.py:401

commit v2 on v1

v2 whole, which is shorter than its diff:
```python
import functools

import jax
import jax.numpy as jnp
from jax import lax
from jax.experimental import pallas as pl
from jax.experimental.pallas import tpu as pltpu
from jax.sharding import PartitionSpec as P

MESH = pl.DeviceIdType.MESH
F32, BF16 = jnp.float32, jnp.bfloat16

NX, NY, NZ, NC = 4, 4, 8, 2
LANES, WIDTH = 32, 16384
BLOCK = 512
YC = 384
ZC = BLOCK - YC
ROWS = 16


def place():
    row, col = lax.axis_index("row"), lax.axis_index("col")
    return col // NC, row // NZ, lax.rem(row, NZ), lax.rem(col, NC)


def device(x, y, z, c):
    return (y * NZ + z, x * NC + c)


def scale_of(total, count):
    return jnp.sqrt(total / count + 1e-06)


def total_of(values):
    return jnp.sum(jnp.sum(values, axis=0, keepdims=True), axis=1, keepdims=True)


def compress(values):
    scale = scale_of(total_of(values * values), values.size)
    packed = (scale * jnp.tanh(values * (3.0 / scale))).astype(BF16)
    return packed, values - packed.astype(F32)


def partners():
    found = [(0, d, 0, 0) for d in range(1, NY)]
    found += [(0, 0, d, 0) for d in range(1, NZ)]
    found += [(dx, 0, 0, dc) for dx in range(NX) for dc in range(NC) if dx or dc]
    found += [(dx, dy, 0, 0) for dx in range(1, NX) for dy in range(1, NY)]
    return found


def fused(
    ctx_h, cot_h, w_h, mom_h, we_h, sr_h, sc_h,
    avg_h, wn_h, ig_h, rn_h, cn_h,
    ctx, cot, w, mom, we, sr, sc, ctx_t, grad, avg, vals, ig, rn, cn,
    send_y, got_y, send_z, got_z, part_y, got_y2, part_z, got_z2, mid, got_c, fin, gat, interleave, pieces,
    in_sem, out_sem, y_s, y_r, z_s, z_r, y2_s, y2_r, z2_s, z2_r, m_s, m_r, f_s, f_r, p_s, p_r, t_s, t_r,
):
    x, y, z, c = place()

    barrier = pltpu.get_barrier_semaphore()
    known = partners()
    for dx, dy, dz, dc in known:
        there = device(lax.rem(x + dx, NX), lax.rem(y + dy, NY), lax.rem(z + dz, NZ), lax.rem(c + dc, NC))
        pl.semaphore_signal(barrier, inc=1, device_id=there, device_id_type=MESH)

    loads = [
        pltpu.make_async_copy(src, dst, in_sem.at[i])
        for i, (src, dst) in enumerate(
            [(ctx_h, ctx), (cot_h, cot), (we_h.at[0, 0], we)]
            + [(mom_h.at[:, pl.ds(128 * k, 128)], mom.at[k]) for k in range(8)]
            + [(w_h, w), (sr_h.at[0, 0], sr), (sc_h.at[0, 0], sc)]
        )
    ]
    for load in loads:
        load.start()

    a = lax.broadcasted_iota(jnp.int32, (256, 256), 0)
    b = lax.broadcasted_iota(jnp.int32, (256, 256), 1)
    interleave[...] = jnp.where(b == lax.rem(a, ROWS) * ROWS + a // ROWS, 1.0, 0.0).astype(BF16)

    loads[0].wait()
    ctx_t[...] = ctx[...].T
    loads[1].wait()

    @pl.loop(0, 4)
    def _(n):
        cols = pl.ds(pl.multiple_of(n * 256, 256), 256)
        product = jnp.dot(ctx_t[...], cot[:, cols], preferred_element_type=F32)
        grad[2 * n] = product[:, :128]
        grad[2 * n + 1] = product[:, 128:]

    total = jnp.zeros((8, 128), F32)
    loads[2].wait()
    for k in range(8):
        loads[3 + k].wait()
        for q in range(ROWS):
            rows = pl.ds(q, LANES, stride=ROWS)
            v = 0.9 * mom[k, rows, :] + 0.1 * grad[k, rows, :] + we[:, 1024 * q + 128 * k : 1024 * q + 128 * k + 128]
            vals[q, :, 128 * k : 128 * k + 128] = v
            v = v * v
            total = total + ((v[0:8] + v[8:16]) + (v[16:24] + v[24:32]))
    scale = scale_of(total_of(total), LANES * WIDTH)
    slope = 3.0 / scale

    def soft(v):
        return (scale * jnp.tanh(v * slope)).astype(BF16)

    pl.semaphore_wait(barrier, len(known))

    def remote(src, dst, sems, at, to):
        copy = pltpu.make_async_remote_copy(
            src_ref=src, dst_ref=dst, send_sem=sems[0].at[at], recv_sem=sems[1].at[at],
            device_id=device(*to), device_id_type=MESH,
        )
        copy.start()
        return copy

    outs = []

    def keep(src, dst):
        copy = pltpu.make_async_copy(src, dst, out_sem.at[len(outs)])
        copy.start()
        outs.append(copy)

    def add(parts):
        total = parts[0].astype(F32)
        for one in parts[1:]:
            total = total + one.astype(F32)
        return total

    order = (2, 1, 3, 0)
    y_copies, z_copies = {}, []

    def along_z(to):
        d = lax.rem(to - z + NZ, NZ)
        z_copies.append(remote(send_z.at[to], got_z.at[z], (z_s, z_r), d, (x, y, to, c)))

    for e in order:
        k = lax.rem(z // 2 + e, NZ // 2)
        for d in order:
            to = lax.rem(y + d, NY)
            q = to * 4 + k
            for half in range(2):
                cols = pl.ds(half * BLOCK, BLOCK)
                v = vals[q, :, cols]
                p = soft(v)
                if d:
                    send_y[to, 2 * k + half] = p[:, :YC]
                else:
                    got_y[y, 2 * k + half] = p[:, :YC]
                send_z[2 * k + half, to] = p[:, YC:]
                vals[q, :, cols] = v - p.astype(F32)
            if d:
                pair = pl.ds(2 * k, 2)
                y_copies[e, d] = remote(
                    send_y.at[to, pair], got_y.at[y, pair], (y_s, y_r), (e, d), (x, to, z, c)
                )
        if e:
            along_z(2 * k)
            along_z(2 * k + 1)
    other = z + 1 - 2 * lax.rem(z, 2)
    along_z(other)
    got_z[z] = send_z[z]
    keep(vals, wn_h)

    y2_copies, z2_copies = [], []

    def sum_y(at):
        return add([got_y[i, at] for i in range(NY)]).astype(BF16)

    def send_part(to):
        part_y[to] = sum_y(to)
        d = lax.rem(to - z + NZ, NZ)
        y2_copies.append(remote(part_y.at[to], got_y2.at[z], (y2_s, y2_r), d, (x, y, to, c)))

    for e in (2, 1, 3):
        for d in (2, 1, 3):
            y_copies[e, d].wait_recv()
        k = lax.rem(z // 2 + e, NZ // 2)
        send_part(2 * k)
        send_part(2 * k + 1)

    far_first = (4, 3, 5, 2, 6, 1, 7)

    def from_z(sems, d, block):
        pltpu.make_async_remote_copy(
            src_ref=block, dst_ref=block, send_sem=sems[0].at[d], recv_sem=sems[1].at[d],
            device_id=device(x, y, lax.rem(z + d, NZ), c), device_id_type=MESH,
        ).wait_recv()

    for d in (2, 1, 3):
        y_copies[0, d].wait_recv()
    send_part(other)
    got_y2[z] = sum_y(z)
    for d in far_first:
        from_z((z_s, z_r), d, got_z.at[0])
    for d in order:
        to = lax.rem(y + d, NY)
        total = add([got_z[i, to] for i in range(NZ)]).astype(BF16)
        if d:
            part_z[to] = total
            z2_copies.append(remote(part_z.at[to], got_z2.at[y], (z2_s, z2_r), d, (x, to, z, c)))
        else:
            got_z2[y] = total

    loads[12].wait()
    loads[13].wait()
    for copy in z2_copies:
        copy.wait_recv()
    for d in far_first:
        from_z((y2_s, y2_r), d, got_y2.at[0])
    first = jnp.concatenate(
        [add([got_y2[i] for i in range(NZ)]), add([got_z2[i] for i in range(NY)])], axis=1
    ) * (1.0 / (NY * NZ)) + sr[...]
    middle, rest = compress(first)

    low = lax.broadcasted_iota(jnp.int32, (ROWS, 128), 1) < 64

    def fold(top, bottom):
        return (
            jnp.where(low, top, pltpu.roll(bottom, 64, axis=1)),
            jnp.where(low, pltpu.roll(top, 64, axis=1), bottom),
        )

    middle = middle.astype(F32)
    for k in range(NX):
        group = middle[:, 128 * k : 128 * k + 128]
        even, odd = fold(group[:16], group[16:])
        mid[2 * k] = even.astype(BF16)
        mid[2 * k + 1] = odd.astype(BF16)
    c_copies = []
    for dx in (2, 1, 3, 0):
        for dc in range(NC):
            if dx or dc:
                tx, tc = lax.rem(x + dx, NX), lax.rem(c + dc, NC)
                c_copies.append(
                    remote(mid.at[2 * tx + tc], got_c.at[2 * x + c], (m_s, m_r), 2 * dx + dc, (tx, y, z, tc))
                )
    got_c[2 * x + c] = mid[2 * x + c]
    rn[...] = rest
    keep(rn, rn_h)
    side = jnp.concatenate([sc[0:16, :], sc[16:32, :]], axis=1)
    for copy in c_copies:
        copy.wait_recv()
    second = add([got_c[i] for i in range(NX * NC)]) * (1.0 / (NX * NC)) + side
    final, rest = compress(second)

    fin[...] = final
    f_copies = [
        remote(fin, gat.at[c, y, x, z], (f_s, f_r), d, (x, y, lax.rem(z + d, NZ), c)) for d in far_first
    ]
    gat[c, y, x, z] = final
    loads[11].wait()
    for i in range(4):
        rows = pl.ds(256 * i, 256)
        ig[rows, :] = lax.dot_general(
            cot[rows, :], w[...], (((1,), (1,)), ((), ())), preferred_element_type=F32
        ).astype(BF16)
    keep(ig, ig_h)
    cn[0:16, :] = rest[:, 0:64]
    cn[16:32, :] = pltpu.roll(rest, 64, axis=1)[:, 0:64]
    keep(cn, cn_h)
    nearest = sorted(
        [(dx, dy) for dx in range(NX) for dy in range(NY)],
        key=lambda d: min(d[0], NX - d[0]) + min(d[1], NY - d[1]),
    )
    p_copies, t_copies = {}, {}
    mine = z // 4

    def part_of(near):
        return pl.ds(4 * mine if near else 4 - 4 * mine, 4)

    def to_plane(near):
        block = gat.at[c, y, x, part_of(near)]
        for dx, dy in nearest[:0:-1]:
            there = (lax.rem(x + dx, NX), lax.rem(y + dy, NY), z, c)
            p_copies[near, dx, dy] = remote(block, block, (p_s, p_r), (near, dx, dy), there)

    def to_sibling(near, dx, dy):
        if dx or dy:
            p_copies[near, dx, dy].wait_recv()
        sx, sy = lax.rem(x - dx + NX, NX), lax.rem(y - dy + NY, NY)
        block = gat.at[c, sy, sx, part_of(near)]
        t_copies[near, dx, dy] = remote(block, block, (t_s, t_r), (near, dx, dy), (x, y, z, 1 - c))

    def unpack(near, dx, dy):
        sx, sy = lax.rem(x - dx + NX, NX), lax.rem(y - dy + NY, NY)
        t_copies[near, dx, dy].wait_recv()
        for i in range(4):
            base = mine if near else 1 - mine
            sz = 4 * base + i
            halves = fold(gat[0, sy, sx, sz].astype(F32), gat[1, sy, sx, sz].astype(F32))
            rows = pl.ds(pl.multiple_of(sy * 64 + base * 32 + i // 2 * 16, 16), 16)
            for h in range(2):
                pieces[h, dx, rows, pl.ds(i % 2 * 128, 128)] = halves[h].astype(BF16)
        if dy == 2 and not near:
            for h in range(2):
                total = jnp.dot(interleave[...], pieces[h, dx], preferred_element_type=F32)
                for side in range(2):
                    avg[4 * side + sx, pl.ds(256 * h, 256), :] = total[:, 128 * side : 128 * side + 128]
            keep(avg.at[sx], avg_h.at[sx])
            keep(avg.at[4 + sx], avg_h.at[4 + sx])

    def piece_from(at):
        d = lax.rem(z - at + NZ, NZ)
        pltpu.make_async_remote_copy(
            src_ref=fin, dst_ref=gat.at[c, y, x, 0], send_sem=f_s.at[d], recv_sem=f_r.at[d],
            device_id=device(x, y, lax.rem(z + d, NZ), c), device_id_type=MESH,
        ).wait_recv()

    for i in range(1, 4):
        piece_from(4 * mine + lax.rem(z + i, 4))
    to_plane(1)
    for i in range(4):
        piece_from(4 - 4 * mine + i)
    to_plane(0)
    for at in nearest:
        to_sibling(1, *at)
    for at in nearest:
        to_sibling(0, *at)
        unpack(1, *at)
    for at in nearest:
        unpack(0, *at)

    sent = list(y_copies.values()) + z_copies + y2_copies + z2_copies + c_copies + f_copies
    for copy in sent + list(p_copies.values()) + list(t_copies.values()):
        copy.wait_send()
    for copy in outs:
        copy.wait()


def finish(avg, wn, ig, rn, cn, avg_out, wn_out, ig_out, rn_out, cn_out, sem):
    moves = [(ig, ig_out), (rn, rn_out.at[0, 0]), (cn, cn_out.at[0, 0])]
    moves += [(wn.at[q], wn_out.at[0, 0, :, pl.ds(1024 * q, 1024)]) for q in range(ROWS)]
    moves += [(avg.at[k], avg_out.at[:, pl.ds(128 * k, 128)]) for k in range(8)]
    copies = [pltpu.make_async_copy(src, dst, sem.at[i]) for i, (src, dst) in enumerate(moves)]
    for copy in copies:
        copy.start()
    for copy in copies:
        copy.wait()


def local(context, cotangent, out_weight, momentum, worker_error, server_rows, server_cols):
    anywhere = pl.BlockSpec(memory_space=pl.ANY)
    dma = pltpu.SemaphoreType.DMA
    args = (context, cotangent, out_weight, momentum, worker_error, server_rows, server_cols)
    held = pl.pallas_call(
        fused,
        out_shape=(
            pltpu.VMEM((8, 512, 128), F32),
            pltpu.VMEM((ROWS, LANES, 1024), F32),
            pltpu.VMEM((1024, 512), BF16),
            pltpu.VMEM((LANES, BLOCK), F32),
            pltpu.VMEM((LANES, 64), F32),
        ),
        in_specs=[anywhere] * 7,
        out_specs=[anywhere] * 5,
        scratch_shapes=[
            pltpu.VMEM((1024, 512), BF16),
            pltpu.VMEM((1024, 1024), BF16),
            pltpu.VMEM((512, 1024), BF16),
            pltpu.VMEM((8, 512, 128), F32),
            pltpu.VMEM((LANES, WIDTH), F32),
            pltpu.VMEM((LANES, BLOCK), F32),
            pltpu.VMEM((LANES, 64), F32),
            pltpu.VMEM((512, 1024), BF16),
            pltpu.VMEM((8, 512, 128), F32),
            pltpu.VMEM((8, 512, 128), F32),
            pltpu.VMEM((ROWS, LANES, 1024), F32),
            pltpu.VMEM((1024, 512), BF16),
            pltpu.VMEM((LANES, BLOCK), F32),
            pltpu.VMEM((LANES, 64), F32),
            pltpu.VMEM((NY, NZ, LANES, YC), BF16),
            pltpu.VMEM((NY, NZ, LANES, YC), BF16),
            pltpu.VMEM((NZ, NY, LANES, ZC), BF16),
            pltpu.VMEM((NZ, NY, LANES, ZC), BF16),
            pltpu.VMEM((NZ, LANES, YC), BF16),
            pltpu.VMEM((NZ, LANES, YC), BF16),
            pltpu.VMEM((NY, LANES, ZC), BF16),
            pltpu.VMEM((NY, LANES, ZC), BF16),
            pltpu.VMEM((NX * NC, 16, 128), BF16),
            pltpu.VMEM((NX * NC, 16, 128), BF16),
            pltpu.VMEM((16, 128), BF16),
            pltpu.VMEM((NC, NY, NX, NZ, 16, 128), BF16),
            pltpu.VMEM((256, 256), BF16),
            pltpu.VMEM((2, NX, 256, 256), BF16),
            dma((14,)), dma((12,)),
            dma((4, NY)), dma((4, NY)), dma((NZ,)), dma((NZ,)), dma((NZ,)), dma((NZ,)), dma((NY,)), dma((NY,)),
            dma((NX * NC,)), dma((NX * NC,)), dma((NZ,)), dma((NZ,)),
            dma((2, NX, NY)), dma((2, NX, NY)), dma((2, NX, NY)), dma((2, NX, NY)),
        ],
        compiler_params=pltpu.CompilerParams(
            collective_id=0, has_side_effects=True, vmem_limit_bytes=44 << 20
        ),
        cost_estimate=pl.CostEstimate(flops=2 << 30, bytes_accessed=13 << 20, transcendentals=1 << 19),
        name="fused",
    )(*[pltpu.with_memory_space_constraint(arg, pltpu.HBM) for arg in args])
    return pl.pallas_call(
        finish,
        out_shape=(
            jax.ShapeDtypeStruct((512, 1024), F32),
            jax.ShapeDtypeStruct((1, 1, LANES, WIDTH), F32),
            jax.ShapeDtypeStruct((1024, 512), BF16),
            jax.ShapeDtypeStruct((1, 1, LANES, BLOCK), F32),
            jax.ShapeDtypeStruct((1, 1, LANES, 64), F32),
        ),
        in_specs=[anywhere] * 5,
        out_specs=[anywhere] * 5,
        scratch_shapes=[dma((27,))],
        compiler_params=pltpu.CompilerParams(vmem_limit_bytes=16 << 20),
        cost_estimate=pl.CostEstimate(flops=0, bytes_accessed=5 << 20, transcendentals=0),
        name="finish",
    )(*held)


def solution(mesh):
    state = P("row", "col", None, None)
    tokens = P(("row", "col"), None)

    def body(*args):
        avg, wn, ig, rn, cn = local(*args)
        return ig, avg, wn, rn, cn

    return jax.shard_map(
        body,
        mesh=mesh,
        in_specs=(tokens, tokens, P(), P(), state, state, state),
        out_specs=(tokens, P(), state, state, state),
        check_vma=False,
    )
```

time: 56.4 us -> 51.4 us (0.911)
  Pallas kernels: 55.5 us -> 50.7 us
    pallas_call x2, Pallas kernels: 55.5 us -> 50.7 us  [the longest x1 48.1 us: local(): pl.pallas_call(fused, out_shape=(pltpu.VMEM((8, 512, 128), F32), pltpu.VM...]
where the time goes in v2:
time: 51.4 us; the launch traced here: 51.3 us
  Pallas kernels  50.7 us (99%)
  between operations  0.64 us (1%)
    pallas_call x1, Pallas kernels, local(): pl.pallas_call(fused, out_shape=(pltpu.VMEM((8, 512, 128), F32), pltpu.VM...  48.1 us
    pallas_call x1, Pallas kernels, local(): pl.pallas_call(finish, out_shape=(jax.ShapeDtypeStruct((512, 1024), F32),...  2.58 us

profile of v2, /device:TPU:1, one launch (start us, length us, event | category | flops | bytes accessed | tf_op | source)
XLA Modules:
  0.0 51.3 jit_solution(12280603043976753252)
XLA Ops:
  0.6 48.1 %fused.1 = (f32[8,512,128]{2,1,0:T(8,128)S(1)}, f32[16,32,1024]{2,1,0:T(8,128)S(1)}, bf16[1024,512]{1,0:T(8,128)(2,1)S(1)}, f32[32,512]{1,0:T(8,128)S(1)}, f32[32,64]{1,0:T(8,128)S(1)}) custom-call(bf16[1024,512]{1,0:T(8,128)(2,1)} %ctx_h.1, bf16[1024,1024]{1,0:T(8,128)(2,1)} %cot_h.1, bf16[512,1024]{1,0:T(8,128)(2,1)} %w_h.1, f32[512,1024]{1,0:T(8,128)} %mom_h.1, ...), custom_call_target="tpu_custom_call" | custom-call | flops 2147483648 | bytes 13631488 | tf_op jit(solution)/shard_map/fused/pallas_call | solution.py:348
  48.8 2.6 %finish.1 = (f32[512,1024]{1,0:T(8,128)}, f32[1,1,32,16384]{3,2,1,0:T(8,128)}, bf16[1024,512]{1,0:T(8,128)(2,1)}, f32[1,1,32,512]{3,2,1,0:T(8,128)}, f32[1,1,32,64]{3,2,1,0:T(8,128)}) custom-call(f32[8,512,128]{2,1,0:T(8,128)S(1)} %get-tuple-element.15.avg, f32[16,32,1024]{2,1,0:T(8,128)S(1)} %get-tuple-element.16.wn, ...), custom_call_target="tpu_custom_call" | custom-call | bytes 5242880 | tf_op jit(solution)/shard_map/finish/pallas_call | solution.py:399

commit v3 on v2

--- a/solution.py
+++ b/solution.py
@@ -35,9 +35,13 @@
     return jnp.sum(jnp.sum(values, axis=0, keepdims=True), axis=1, keepdims=True)
 
 
+def soft(values, scale, slope):
+    return (scale * jnp.tanh(values * slope)).astype(BF16)
+
+
 def compress(values):
     scale = scale_of(total_of(values * values), values.size)
-    packed = (scale * jnp.tanh(values * (3.0 / scale))).astype(BF16)
+    packed = soft(values, scale, 3.0 / scale)
     return packed, values - packed.astype(F32)
 
 
@@ -58,21 +62,24 @@
 ):
     x, y, z, c = place()
 
+    loads = [
+        pltpu.make_async_copy(src, dst, in_sem.at[i])
+        for i, (src, dst) in enumerate(
+            [(ctx_h, ctx), (cot_h.at[:, pl.ds(0, 512)], cot.at[:, pl.ds(0, 512)]), (we_h.at[0, 0], we)]
+            + [(mom_h.at[:, pl.ds(128 * k, 128)], mom.at[k]) for k in range(8)]
+            + [(w_h, w), (sr_h.at[0, 0], sr), (sc_h.at[0, 0], sc), (cot_h.at[:, pl.ds(512, 512)], cot.at[:, pl.ds(512, 512)])]
+        )
+    ]
+    for load in loads[:2] + loads[14:]:
+        load.start()
+
     barrier = pltpu.get_barrier_semaphore()
     known = partners()
     for dx, dy, dz, dc in known:
         there = device(lax.rem(x + dx, NX), lax.rem(y + dy, NY), lax.rem(z + dz, NZ), lax.rem(c + dc, NC))
         pl.semaphore_signal(barrier, inc=1, device_id=there, device_id_type=MESH)
 
-    loads = [
-        pltpu.make_async_copy(src, dst, in_sem.at[i])
-        for i, (src, dst) in enumerate(
-            [(ctx_h, ctx), (cot_h, cot), (we_h.at[0, 0], we)]
-            + [(mom_h.at[:, pl.ds(128 * k, 128)], mom.at[k]) for k in range(8)]
-            + [(w_h, w), (sr_h.at[0, 0], sr), (sc_h.at[0, 0], sc)]
-        )
-    ]
-    for load in loads:
+    for load in loads[2:14]:
         load.start()
 
     a = lax.broadcasted_iota(jnp.int32, (256, 256), 0)
@@ -83,10 +90,10 @@
     ctx_t[...] = ctx[...].T
     loads[1].wait()
 
-    @pl.loop(0, 4)
-    def _(n):
-        cols = pl.ds(pl.multiple_of(n * 256, 256), 256)
-        product = jnp.dot(ctx_t[...], cot[:, cols], preferred_element_type=F32)
+    for n in range(4):
+        if n == 2:
+            loads[14].wait()
+        product = jnp.dot(ctx_t[...], cot[:, 256 * n : 256 * n + 256], preferred_element_type=F32)
         grad[2 * n] = product[:, :128]
         grad[2 * n + 1] = product[:, 128:]
 
@@ -103,9 +110,6 @@
     scale = scale_of(total_of(total), LANES * WIDTH)
     slope = 3.0 / scale
 
-    def soft(v):
-        return (scale * jnp.tanh(v * slope)).astype(BF16)
-
     pl.semaphore_wait(barrier, len(known))
 
     def remote(src, dst, sems, at, to):
@@ -144,7 +148,7 @@
             for half in range(2):
                 cols = pl.ds(half * BLOCK, BLOCK)
                 v = vals[q, :, cols]
-                p = soft(v)
+                p = soft(v, scale, slope)
                 if d:
                     send_y[to, 2 * k + half] = p[:, :YC]
                 else:
@@ -213,8 +217,6 @@
     first = jnp.concatenate(
         [add([got_y2[i] for i in range(NZ)]), add([got_z2[i] for i in range(NY)])], axis=1
     ) * (1.0 / (NY * NZ)) + sr[...]
-    middle, rest = compress(first)
-
     low = lax.broadcasted_iota(jnp.int32, (ROWS, 128), 1) < 64
 
     def fold(top, bottom):
@@ -223,12 +225,12 @@
             jnp.where(low, pltpu.roll(top, 64, axis=1), bottom),
         )
 
-    middle = middle.astype(F32)
+    folded = [fold(first[:16, 128 * k : 128 * k + 128], first[16:, 128 * k : 128 * k + 128]) for k in range(NX)]
+    scale = scale_of(total_of(first * first), LANES * BLOCK)
+    slope = 3.0 / scale
     for k in range(NX):
-        group = middle[:, 128 * k : 128 * k + 128]
-        even, odd = fold(group[:16], group[16:])
-        mid[2 * k] = even.astype(BF16)
-        mid[2 * k + 1] = odd.astype(BF16)
+        for h in range(NC):
+            mid[2 * k + h] = soft(folded[k][h], scale, slope)
     c_copies = []
     for dx in (2, 1, 3, 0):
         for dc in range(NC):
@@ -238,7 +240,7 @@
                     remote(mid.at[2 * tx + tc], got_c.at[2 * x + c], (m_s, m_r), 2 * dx + dc, (tx, y, z, tc))
                 )
     got_c[2 * x + c] = mid[2 * x + c]
-    rn[...] = rest
+    rn[...] = first - soft(first, scale, slope).astype(F32)
     keep(rn, rn_h)
     side = jnp.concatenate([sc[0:16, :], sc[16:32, :]], axis=1)
     for copy in c_copies:
@@ -385,7 +387,7 @@
             pltpu.VMEM((NC, NY, NX, NZ, 16, 128), BF16),
             pltpu.VMEM((256, 256), BF16),
             pltpu.VMEM((2, NX, 256, 256), BF16),
-            dma((14,)), dma((12,)),
+            dma((15,)), dma((12,)),
             dma((4, NY)), dma((4, NY)), dma((NZ,)), dma((NZ,)), dma((NZ,)), dma((NZ,)), dma((NY,)), dma((NY,)),
             dma((NX * NC,)), dma((NX * NC,)), dma((NZ,)), dma((NZ,)),
             dma((2, NX, NY)), dma((2, NX, NY)), dma((2, NX, NY)), dma((2, NX, NY)),

time: 51.4 us -> 50 us (0.973)
  Pallas kernels: 50.7 us -> 49.2 us
    pallas_call x1, Pallas kernels: 48.1 us -> 46.7 us  [local(): pl.pallas_call(fused, out_shape=(pltpu.VMEM((8, 512, 128), F32), pltpu.VM...]
where the time goes in v3:
time: 50 us; the launch traced here: 49.9 us
  Pallas kernels  49.2 us (98%)
  between operations  0.64 us (1%)
    pallas_call x1, Pallas kernels, local(): pl.pallas_call(fused, out_shape=(pltpu.VMEM((8, 512, 128), F32), pltpu.VM...  46.7 us
    pallas_call x1, Pallas kernels, local(): pl.pallas_call(finish, out_shape=(jax.ShapeDtypeStruct((512, 1024), F32),...  2.58 us

profile of v3, /device:TPU:1, one launch (start us, length us, event | category | flops | bytes accessed | tf_op | source)
XLA Modules:
  0.0 49.9 jit_solution(8301968990632127990)
XLA Ops:
  0.6 46.7 %fused.1 = (f32[8,512,128]{2,1,0:T(8,128)S(1)}, f32[16,32,1024]{2,1,0:T(8,128)S(1)}, bf16[1024,512]{1,0:T(8,128)(2,1)S(1)}, f32[32,512]{1,0:T(8,128)S(1)}, f32[32,64]{1,0:T(8,128)S(1)}) custom-call(bf16[1024,512]{1,0:T(8,128)(2,1)} %ctx_h.1, bf16[1024,1024]{1,0:T(8,128)(2,1)} %cot_h.1, bf16[512,1024]{1,0:T(8,128)(2,1)} %w_h.1, f32[512,1024]{1,0:T(8,128)} %mom_h.1, ...), custom_call_target="tpu_custom_call" | custom-call | flops 2147483648 | bytes 13631488 | tf_op jit(solution)/shard_map/fused/pallas_call | solution.py:350
  47.3 2.6 %finish.1 = (f32[512,1024]{1,0:T(8,128)}, f32[1,1,32,16384]{3,2,1,0:T(8,128)}, bf16[1024,512]{1,0:T(8,128)(2,1)}, f32[1,1,32,512]{3,2,1,0:T(8,128)}, f32[1,1,32,64]{3,2,1,0:T(8,128)}) custom-call(f32[8,512,128]{2,1,0:T(8,128)S(1)} %get-tuple-element.15.avg, f32[16,32,1024]{2,1,0:T(8,128)S(1)} %get-tuple-element.16.wn, ...), custom_call_target="tpu_custom_call" | custom-call | bytes 5242880 | tf_op jit(solution)/shard_map/finish/pallas_call | solution.py:401

commit v4 on v3

--- a/solution.py
+++ b/solution.py
@@ -57,7 +57,7 @@
     ctx_h, cot_h, w_h, mom_h, we_h, sr_h, sc_h,
     avg_h, wn_h, ig_h, rn_h, cn_h,
     ctx, cot, w, mom, we, sr, sc, ctx_t, grad, avg, vals, ig, rn, cn,
-    send_y, got_y, send_z, got_z, part_y, got_y2, part_z, got_z2, mid, got_c, fin, gat, interleave, pieces,
+    send_y, got_y, send_z, got_z, part_y, got_y2, part_z, got_z2, mid, got_c, fin, gat,
     in_sem, out_sem, y_s, y_r, z_s, z_r, y2_s, y2_r, z2_s, z2_r, m_s, m_r, f_s, f_r, p_s, p_r, t_s, t_r,
 ):
     x, y, z, c = place()
@@ -79,12 +79,8 @@
         there = device(lax.rem(x + dx, NX), lax.rem(y + dy, NY), lax.rem(z + dz, NZ), lax.rem(c + dc, NC))
         pl.semaphore_signal(barrier, inc=1, device_id=there, device_id_type=MESH)
 
-    for load in loads[2:14]:
+    for load in loads[3:11] + loads[2:3] + loads[11:14]:
         load.start()
-
-    a = lax.broadcasted_iota(jnp.int32, (256, 256), 0)
-    b = lax.broadcasted_iota(jnp.int32, (256, 256), 1)
-    interleave[...] = jnp.where(b == lax.rem(a, ROWS) * ROWS + a // ROWS, 1.0, 0.0).astype(BF16)
 
     loads[0].wait()
     ctx_t[...] = ctx[...].T
@@ -97,13 +93,14 @@
         grad[2 * n] = product[:, :128]
         grad[2 * n + 1] = product[:, 128:]
 
+    for k in range(8):
+        loads[3 + k].wait()
+        grad[k] = 0.9 * mom[k] + 0.1 * grad[k]
     total = jnp.zeros((8, 128), F32)
     loads[2].wait()
-    for k in range(8):
-        loads[3 + k].wait()
-        for q in range(ROWS):
-            rows = pl.ds(q, LANES, stride=ROWS)
-            v = 0.9 * mom[k, rows, :] + 0.1 * grad[k, rows, :] + we[:, 1024 * q + 128 * k : 1024 * q + 128 * k + 128]
+    for q in range(ROWS):
+        for k in range(8):
+            v = grad[k, pl.ds(q, LANES, stride=ROWS), :] + we[:, 1024 * q + 128 * k : 1024 * q + 128 * k + 128]
             vals[q, :, 128 * k : 128 * k + 128] = v
             v = v * v
             total = total + ((v[0:8] + v[8:16]) + (v[16:24] + v[24:32]))
@@ -126,6 +123,10 @@
         copy = pltpu.make_async_copy(src, dst, out_sem.at[len(outs)])
         copy.start()
         outs.append(copy)
+
+    def finished(copies):
+        for copy in copies:
+            copy.wait_send()
 
     def add(parts):
         total = parts[0].astype(F32)
@@ -208,6 +209,7 @@
         else:
             got_z2[y] = total
 
+    finished(list(y_copies.values()) + z_copies)
     loads[12].wait()
     loads[13].wait()
     for copy in z2_copies:
@@ -217,12 +219,13 @@
     first = jnp.concatenate(
         [add([got_y2[i] for i in range(NZ)]), add([got_z2[i] for i in range(NY)])], axis=1
     ) * (1.0 / (NY * NZ)) + sr[...]
-    low = lax.broadcasted_iota(jnp.int32, (ROWS, 128), 1) < 64
+    def low_of(half):
+        return lax.broadcasted_iota(jnp.int32, half.shape, 1) < 64
 
     def fold(top, bottom):
         return (
-            jnp.where(low, top, pltpu.roll(bottom, 64, axis=1)),
-            jnp.where(low, pltpu.roll(top, 64, axis=1), bottom),
+            jnp.where(low_of(top), top, pltpu.roll(bottom, 64, axis=1)),
+            jnp.where(low_of(top), pltpu.roll(top, 64, axis=1), bottom),
         )
 
     folded = [fold(first[:16, 128 * k : 128 * k + 128], first[16:, 128 * k : 128 * k + 128]) for k in range(NX)]
@@ -243,6 +246,7 @@
     rn[...] = first - soft(first, scale, slope).astype(F32)
     keep(rn, rn_h)
     side = jnp.concatenate([sc[0:16, :], sc[16:32, :]], axis=1)
+    finished(y2_copies + z2_copies)
     for copy in c_copies:
         copy.wait_recv()
     second = add([got_c[i] for i in range(NX * NC)]) * (1.0 / (NX * NC)) + side
@@ -250,9 +254,9 @@
 
     fin[...] = final
     f_copies = [
-        remote(fin, gat.at[c, y, x, z], (f_s, f_r), d, (x, y, lax.rem(z + d, NZ), c)) for d in far_first
+        remote(fin, gat.at[c, x, lax.rem(z, 2), y, z // 2], (f_s, f_r), d, (x, y, lax.rem(z + d, NZ), c)) for d in far_first
     ]
-    gat[c, y, x, z] = final
+    gat[c, x, lax.rem(z, 2), y, z // 2] = final
     loads[11].wait()
     for i in range(4):
         rows = pl.ds(256 * i, 256)
@@ -271,10 +275,10 @@
     mine = z // 4
 
     def part_of(near):
-        return pl.ds(4 * mine if near else 4 - 4 * mine, 4)
+        return pl.ds(2 * mine if near else 2 - 2 * mine, 2)
 
     def to_plane(near):
-        block = gat.at[c, y, x, part_of(near)]
+        block = gat.at[c, x, :, y, part_of(near)]
         for dx, dy in nearest[:0:-1]:
             there = (lax.rem(x + dx, NX), lax.rem(y + dy, NY), z, c)
             p_copies[near, dx, dy] = remote(block, block, (p_s, p_r), (near, dx, dy), there)
@@ -283,52 +287,50 @@
         if dx or dy:
             p_copies[near, dx, dy].wait_recv()
         sx, sy = lax.rem(x - dx + NX, NX), lax.rem(y - dy + NY, NY)
-        block = gat.at[c, sy, sx, part_of(near)]
+        block = gat.at[c, sx, :, sy, part_of(near)]
         t_copies[near, dx, dy] = remote(block, block, (t_s, t_r), (near, dx, dy), (x, y, z, 1 - c))
 
-    def unpack(near, dx, dy):
-        sx, sy = lax.rem(x - dx + NX, NX), lax.rem(y - dy + NY, NY)
-        t_copies[near, dx, dy].wait_recv()
-        for i in range(4):
-            base = mine if near else 1 - mine
-            sz = 4 * base + i
-            halves = fold(gat[0, sy, sx, sz].astype(F32), gat[1, sy, sx, sz].astype(F32))
-            rows = pl.ds(pl.multiple_of(sy * 64 + base * 32 + i // 2 * 16, 16), 16)
-            for h in range(2):
-                pieces[h, dx, rows, pl.ds(i % 2 * 128, 128)] = halves[h].astype(BF16)
-        if dy == 2 and not near:
-            for h in range(2):
-                total = jnp.dot(interleave[...], pieces[h, dx], preferred_element_type=F32)
-                for side in range(2):
-                    avg[4 * side + sx, pl.ds(256 * h, 256), :] = total[:, 128 * side : 128 * side + 128]
-            keep(avg.at[sx], avg_h.at[sx])
-            keep(avg.at[4 + sx], avg_h.at[4 + sx])
+    def unpack(dx):
+        sx = lax.rem(x - dx + NX, NX)
+        for h in range(2):
+            for sy in range(NY):
+                for i in range(NZ // 2):
+                    halves = fold(gat[0, sx, h, sy, i], gat[1, sx, h, sy, i])
+                    for side in range(2):
+                        rows = pl.ds(256 * side + 4 * sy + i, 16, stride=ROWS)
+                        avg[4 * h + sx, rows, :] = halves[side].astype(F32)
+            keep(avg.at[4 * h + sx], avg_h.at[4 * h + sx])
 
     def piece_from(at):
         d = lax.rem(z - at + NZ, NZ)
         pltpu.make_async_remote_copy(
-            src_ref=fin, dst_ref=gat.at[c, y, x, 0], send_sem=f_s.at[d], recv_sem=f_r.at[d],
+            src_ref=fin, dst_ref=gat.at[c, x, 0, y, 0], send_sem=f_s.at[d], recv_sem=f_r.at[d],
             device_id=device(x, y, lax.rem(z + d, NZ), c), device_id_type=MESH,
         ).wait_recv()
 
+    finished(c_copies)
     for i in range(1, 4):
         piece_from(4 * mine + lax.rem(z + i, 4))
     to_plane(1)
     for i in range(4):
         piece_from(4 - 4 * mine + i)
     to_plane(0)
+    finished(f_copies)
+    for copy in outs[:4]:
+        copy.wait()
     for at in nearest:
         to_sibling(1, *at)
     for at in nearest:
         to_sibling(0, *at)
-        unpack(1, *at)
-    for at in nearest:
-        unpack(0, *at)
-
-    sent = list(y_copies.values()) + z_copies + y2_copies + z2_copies + c_copies + f_copies
-    for copy in sent + list(p_copies.values()) + list(t_copies.values()):
-        copy.wait_send()
-    for copy in outs:
+    finished([p_copies[1, dx, dy] for dx, dy in nearest[1:]])
+    for dx in (0, 1, 3, 2):
+        for near in (1, 0):
+            for dy in range(NY):
+                t_copies[near, dx, dy].wait_recv()
+        unpack(dx)
+    finished([p_copies[0, dx, dy] for dx, dy in nearest[1:]] + [t_copies[1, dx, dy] for dx, dy in nearest])
+    finished([t_copies[0, dx, dy] for dx, dy in nearest])
+    for copy in outs[4:]:
         copy.wait()
 
 
@@ -384,9 +386,7 @@
             pltpu.VMEM((NX * NC, 16, 128), BF16),
             pltpu.VMEM((NX * NC, 16, 128), BF16),
             pltpu.VMEM((16, 128), BF16),
-            pltpu.VMEM((NC, NY, NX, NZ, 16, 128), BF16),
-            pltpu.VMEM((256, 256), BF16),
-            pltpu.VMEM((2, NX, 256, 256), BF16),
+            pltpu.VMEM((NC, NX, 2, NY, NZ // 2, 16, 128), BF16),
             dma((15,)), dma((12,)),
             dma((4, NY)), dma((4, NY)), dma((NZ,)), dma((NZ,)), dma((NZ,)), dma((NZ,)), dma((NY,)), dma((NY,)),
             dma((NX * NC,)), dma((NX * NC,)), dma((NZ,)), dma((NZ,)),

time: 50 us -> 49.1 us (0.982)
  Pallas kernels: 49.2 us -> 48.3 us
    pallas_call x1, Pallas kernels: 46.7 us -> 45.8 us  [local(): pl.pallas_call(fused, out_shape=(pltpu.VMEM((8, 512, 128), F32), pltpu.VM...]
where the time goes in v4:
time: 49.1 us; the launch traced here: 49 us
  Pallas kernels  48.3 us (98%)
  between operations  0.64 us (1%)
    pallas_call x1, Pallas kernels, local(): pl.pallas_call(fused, out_shape=(pltpu.VMEM((8, 512, 128), F32), pltpu.VM...  45.8 us
    pallas_call x1, Pallas kernels, local(): pl.pallas_call(finish, out_shape=(jax.ShapeDtypeStruct((512, 1024), F32),...  2.58 us

profile of v4, /device:TPU:1, one launch (start us, length us, event | category | flops | bytes accessed | tf_op | source)
XLA Modules:
  0.0 49.0 jit_solution(11456928934858338235)
XLA Ops:
  0.6 45.8 %fused.1 = (f32[8,512,128]{2,1,0:T(8,128)S(1)}, f32[16,32,1024]{2,1,0:T(8,128)S(1)}, bf16[1024,512]{1,0:T(8,128)(2,1)S(1)}, f32[32,512]{1,0:T(8,128)S(1)}, f32[32,64]{1,0:T(8,128)S(1)}) custom-call(bf16[1024,512]{1,0:T(8,128)(2,1)} %ctx_h.1, bf16[1024,1024]{1,0:T(8,128)(2,1)} %cot_h.1, bf16[512,1024]{1,0:T(8,128)(2,1)} %w_h.1, f32[512,1024]{1,0:T(8,128)} %mom_h.1, ...), custom_call_target="tpu_custom_call" | custom-call | flops 2147483648 | bytes 13631488 | tf_op jit(solution)/shard_map/fused/pallas_call | solution.py:352
  46.4 2.6 %finish.1 = (f32[512,1024]{1,0:T(8,128)}, f32[1,1,32,16384]{3,2,1,0:T(8,128)}, bf16[1024,512]{1,0:T(8,128)(2,1)}, f32[1,1,32,512]{3,2,1,0:T(8,128)}, f32[1,1,32,64]{3,2,1,0:T(8,128)}) custom-call(f32[8,512,128]{2,1,0:T(8,128)S(1)} %get-tuple-element.15.avg, f32[16,32,1024]{2,1,0:T(8,128)S(1)} %get-tuple-element.16.wn, ...), custom_call_target="tpu_custom_call" | custom-call | bytes 5242880 | tf_op jit(solution)/shard_map/finish/pallas_call | solution.py:401

commit v5 on v4

--- a/solution.py
+++ b/solution.py
@@ -65,12 +65,13 @@
     loads = [
         pltpu.make_async_copy(src, dst, in_sem.at[i])
         for i, (src, dst) in enumerate(
-            [(ctx_h, ctx), (cot_h.at[:, pl.ds(0, 512)], cot.at[:, pl.ds(0, 512)]), (we_h.at[0, 0], we)]
+            [(ctx_h, ctx), (cot_h.at[:, pl.ds(0, 512)], cot.at[:, pl.ds(0, 512)]), (we_h.at[0, 0, :, pl.ds(0, 4096)], we.at[:, pl.ds(0, 4096)])]
             + [(mom_h.at[:, pl.ds(128 * k, 128)], mom.at[k]) for k in range(8)]
             + [(w_h, w), (sr_h.at[0, 0], sr), (sc_h.at[0, 0], sc), (cot_h.at[:, pl.ds(512, 512)], cot.at[:, pl.ds(512, 512)])]
+            + [(we_h.at[0, 0, :, pl.ds(4096 * i, 4096)], we.at[:, pl.ds(4096 * i, 4096)]) for i in range(1, 4)]
         )
     ]
-    for load in loads[:2] + loads[14:]:
+    for load in loads[:2] + loads[14:15]:
         load.start()
 
     barrier = pltpu.get_barrier_semaphore()
@@ -79,7 +80,7 @@
         there = device(lax.rem(x + dx, NX), lax.rem(y + dy, NY), lax.rem(z + dz, NZ), lax.rem(c + dc, NC))
         pl.semaphore_signal(barrier, inc=1, device_id=there, device_id_type=MESH)
 
-    for load in loads[3:11] + loads[2:3] + loads[11:14]:
+    for load in loads[3:11] + loads[2:3] + loads[15:] + loads[11:14]:
         load.start()
 
     loads[0].wait()
@@ -97,8 +98,9 @@
         loads[3 + k].wait()
         grad[k] = 0.9 * mom[k] + 0.1 * grad[k]
     total = jnp.zeros((8, 128), F32)
-    loads[2].wait()
     for q in range(ROWS):
+        if q % 4 == 0:
+            loads[14 + q // 4 if q else 2].wait()
         for k in range(8):
             v = grad[k, pl.ds(q, LANES, stride=ROWS), :] + we[:, 1024 * q + 128 * k : 1024 * q + 128 * k + 128]
             vals[q, :, 128 * k : 128 * k + 128] = v
@@ -387,7 +389,7 @@
             pltpu.VMEM((NX * NC, 16, 128), BF16),
             pltpu.VMEM((16, 128), BF16),
             pltpu.VMEM((NC, NX, 2, NY, NZ // 2, 16, 128), BF16),
-            dma((15,)), dma((12,)),
+            dma((18,)), dma((12,)),
             dma((4, NY)), dma((4, NY)), dma((NZ,)), dma((NZ,)), dma((NZ,)), dma((NZ,)), dma((NY,)), dma((NY,)),
             dma((NX * NC,)), dma((NX * NC,)), dma((NZ,)), dma((NZ,)),
             dma((2, NX, NY)), dma((2, NX, NY)), dma((2, NX, NY)), dma((2, NX, NY)),

time: 49.1 us -> 49.2 us (level)
  no operation moved by 1% of the time
where the time goes in v5:
time: 49.2 us; the launch traced here: 49.1 us
  Pallas kernels  48.4 us (98%)
  between operations  0.64 us (1%)
    pallas_call x1, Pallas kernels, local(): pl.pallas_call(fused, out_shape=(pltpu.VMEM((8, 512, 128), F32), pltpu.VM...  45.9 us
    pallas_call x1, Pallas kernels, local(): pl.pallas_call(finish, out_shape=(jax.ShapeDtypeStruct((512, 1024), F32),...  2.58 us

profile of v5, /device:TPU:1, one launch (start us, length us, event | category | flops | bytes accessed | tf_op | source)
XLA Modules:
  0.0 49.1 jit_solution(12047300074756125726)
XLA Ops:
  0.6 45.9 %fused.1 = (f32[8,512,128]{2,1,0:T(8,128)S(1)}, f32[16,32,1024]{2,1,0:T(8,128)S(1)}, bf16[1024,512]{1,0:T(8,128)(2,1)S(1)}, f32[32,512]{1,0:T(8,128)S(1)}, f32[32,64]{1,0:T(8,128)S(1)}) custom-call(bf16[1024,512]{1,0:T(8,128)(2,1)} %ctx_h.1, bf16[1024,1024]{1,0:T(8,128)(2,1)} %cot_h.1, bf16[512,1024]{1,0:T(8,128)(2,1)} %w_h.1, f32[512,1024]{1,0:T(8,128)} %mom_h.1, ...), custom_call_target="tpu_custom_call" | custom-call | flops 2147483648 | bytes 13631488 | tf_op jit(solution)/shard_map/fused/pallas_call | solution.py:354
  46.5 2.6 %finish.1 = (f32[512,1024]{1,0:T(8,128)}, f32[1,1,32,16384]{3,2,1,0:T(8,128)}, bf16[1024,512]{1,0:T(8,128)(2,1)}, f32[1,1,32,512]{3,2,1,0:T(8,128)}, f32[1,1,32,64]{3,2,1,0:T(8,128)}) custom-call(f32[8,512,128]{2,1,0:T(8,128)S(1)} %get-tuple-element.15.avg, f32[16,32,1024]{2,1,0:T(8,128)S(1)} %get-tuple-element.16.wn, ...), custom_call_target="tpu_custom_call" | custom-call | bytes 5242880 | tf_op jit(solution)/shard_map/finish/pallas_call | solution.py:403
